TPU v7x, 128 devices: a whole 4x4x4 slice. The times are simulated.
128 devices in a mesh: dp: 16 (over x, z_lo, core), tensor: 8 (over z_hi, y).
Axes of the slice: x: 4, y: 4, z: 4 (z_hi: 2, z_lo: 2; z = z_hi * 2 + z_lo), core: 2. Of those that a mesh axis runs over, the one named last changes fastest.
Arguments:
- tokens: bfloat16 [16384, 3072], P(('dp', 'tensor')), may hold values from -6 to 6
- cotangent: bfloat16 [16384, 3072], P(('dp', 'tensor')), may hold values from -6 to 6
- expert_ids: int32 [16384, 2], P(('dp', 'tensor')), may hold values from 0 to 7, as said below
- combine: float32 [16384], P(('dp', 'tensor')), may hold values from 0.2 to 1
- w_gate: bfloat16 [3072, 8192], P(None, 'tensor'), may hold values from -0.109375 to 0.109375
- w_up: bfloat16 [3072, 8192], P(None, 'tensor'), may hold values from -0.109375 to 0.109375
- w_down: bfloat16 [8192, 3072], P('tensor'), may hold values from -0.0625 to 0.0625
Outputs:
- expert_output: bfloat16 [16384, 3072], P(('dp', 'tensor'))
- token_grad: bfloat16 [16384, 3072], P(('dp', 'tensor'))
- gate_grad: bfloat16 [3072, 8192], P('dp', 'tensor')
- up_grad: bfloat16 [3072, 8192], P('dp', 'tensor')
- down_grad: bfloat16 [8192, 3072], P('tensor', 'dp')
Inputs may be any that keep to these rules, and one draw needn't show every extreme that they name: `expert_ids`: each row names two different experts. Within each aligned block of 128 rows (the rows of one device) expert 0 is named by at most 48 rows, and in every draw all blocks of some group of 1024 rows name it exactly 48 times.
All inputs are finite; a program needn't handle non-finite values.
Results may differ from a plain program's by a relative error of at most 0.022.
Values may be sent and summed in bfloat16 or wider, within the bound.
No kernel may reach another device: no remote copies, remote signals or barrier semaphores. Data moves between devices by JAX's collectives and lax.ppermute only.
A program may use at most 192 MiB of HBM per device.

v0:
```python
import jax
import jax.numpy as jnp
from jax import lax
from jax.sharding import PartitionSpec as P

DEV_CAP = 48


highest = lax.Precision.HIGHEST


def picker(expert_ids, slot_count):
    chosen = jnp.any(expert_ids == 0, axis=1)
    slot_place = jnp.cumsum(chosen.astype(jnp.int32)) - 1
    slot_ids = lax.broadcasted_iota(jnp.int32, (slot_count, expert_ids.shape[0]), 0)
    return jnp.where(chosen[None, :] & (slot_place[None, :] == slot_ids), 1.0, 0.0).astype(
        jnp.float32
    )


def contract_rows(left_rows, right_rows):
    return lax.dot_general(
        left_rows, right_rows, (((0,), (0,)), ((), ())), preferred_element_type=jnp.float32
    )


def times_transpose(left_rows, right_rows):
    return lax.dot_general(
        left_rows, right_rows, (((1,), (1,)), ((), ())), preferred_element_type=jnp.float32
    )


def local(tokens, cotangent, expert_ids, combine, w_gate, w_up, w_down):
    slot_count = DEV_CAP
    picks = picker(expert_ids, slot_count)
    picks_low = picks.astype(jnp.bfloat16)
    d_local = (combine[:, None] * cotangent.astype(jnp.float32)).astype(jnp.bfloat16)
    x_sel = jnp.dot(picks_low, tokens, preferred_element_type=jnp.float32).astype(jnp.bfloat16)
    d_sel = jnp.dot(picks_low, d_local, preferred_element_type=jnp.float32).astype(jnp.bfloat16)
    rows_x, rows_d = (
        lax.all_gather(x_sel, "tensor", axis=0, tiled=True),
        lax.all_gather(d_sel, "tensor", axis=0, tiled=True),
    )
    gate_pre = jnp.dot(rows_x, w_gate, preferred_element_type=jnp.float32)
    up_pre = jnp.dot(rows_x, w_up, preferred_element_type=jnp.float32)
    sigmoid_gate = jax.nn.sigmoid(gate_pre)
    gate_act = gate_pre * sigmoid_gate
    hidden = (gate_act * up_pre).astype(jnp.bfloat16)
    d_hidden = times_transpose(rows_d, w_down)
    d_up = (d_hidden * gate_act).astype(jnp.bfloat16)
    d_gate = (d_hidden * up_pre * sigmoid_gate * (1.0 + gate_pre * (1.0 - sigmoid_gate))).astype(
        jnp.bfloat16
    )
    out_term = jnp.dot(hidden, w_down, preferred_element_type=jnp.float32)
    back_term = times_transpose(d_gate, w_gate) + times_transpose(d_up, w_up)
    out_own, back_own = (
        lax.psum_scatter(
            out_term.astype(jnp.bfloat16), "tensor", scatter_dimension=0, tiled=True
        ).astype(jnp.float32),
        lax.psum_scatter(
            back_term.astype(jnp.bfloat16), "tensor", scatter_dimension=0, tiled=True
        ).astype(jnp.float32),
    )
    placed_out = lax.dot_general(
        picks,
        out_own,
        (((0,), (0,)), ((), ())),
        precision=highest,
        preferred_element_type=jnp.float32,
    )
    placed_back = lax.dot_general(
        picks,
        back_own,
        (((0,), (0,)), ((), ())),
        precision=highest,
        preferred_element_type=jnp.float32,
    )
    expert_output = (combine[:, None] * placed_out).astype(jnp.bfloat16)
    token_grad = placed_back.astype(jnp.bfloat16)
    sum_gate, sum_up, sum_down = (
        lax.psum_scatter(
            contract_rows(rows_x, d_gate).astype(jnp.bfloat16),
            "dp",
            scatter_dimension=0,
            tiled=True,
        ).astype(jnp.float32),
        lax.psum_scatter(
            contract_rows(rows_x, d_up).astype(jnp.bfloat16), "dp", scatter_dimension=0, tiled=True
        ).astype(jnp.float32),
        lax.psum_scatter(
            contract_rows(rows_d, hidden).astype(jnp.bfloat16),
            "dp",
            scatter_dimension=0,
            tiled=True,
        ).astype(jnp.float32),
    )
    gate_grad = sum_gate.astype(jnp.bfloat16)
    up_grad = sum_up.astype(jnp.bfloat16)
    down_grad = sum_down.T.astype(jnp.bfloat16)
    return (expert_output, token_grad, gate_grad, up_grad, down_grad)


def solution(mesh):
    placed = (
        P(("dp", "tensor"), None),
        P(("dp", "tensor"), None),
        P(("dp", "tensor"), None),
        P(("dp", "tensor")),
        P(None, "tensor"),
        P(None, "tensor"),
        P("tensor", None),
    )
    return jax.shard_map(
        local,
        mesh=mesh,
        in_specs=placed,
        out_specs=(
            P(("dp", "tensor"), None),
            P(("dp", "tensor"), None),
            P("dp", "tensor"),
            P("dp", "tensor"),
            P("tensor", "dp"),
        ),
        check_vma=False,
    )
```

profile of v0, /device:TPU:1, one launch (start us, length us, event | category | flops | bytes accessed | tf_op | source)
XLA Modules:
  0.0 548.7 jit_solution(6446471605378046742)
XLA Ops:
  7.2 0.0 copy-start
  7.2 0.0 all-gather.3.cloned.1.call-start
  7.2 0.8 compare_reduce_fusion
  8.0 0.1 copy.13
  8.1 0.2 reduce-window.8
  8.3 0.1 add_reduce_fusion
  8.4 0.0 copy-done
  8.4 1.0 convolution_convert_fusion.6
  9.4 0.0 all-gather.3.cloned.1.call-update
  9.4 0.0 all-gather.5.cloned.1.call-start
  9.4 2.2 convolution_convert_fusion.5
  11.7 0.0 all-gather.5.cloned.1.call-update
  11.7 0.0 reduce-scatter.8.cloned.1.call-start
  11.7 58.4 %all-gather.3.cloned.1.call-done = bf16[384,3072]{1,0:T(8,128)(2,1)} async-done(((bf16[48,3072]{1,0:T(8,128)(2,1)}), bf16[384,3072]{1,0:T(8,128)(2,1)}) %all-gather.3.cloned.1.call-update) | async-done | bytes 2359312 | tf_op jit(solution)/shard_map/all_gather | solution.py:41
  70.1 0.0 copy-start.2
  70.1 7.4 %fusion.33 = f32[384,1024]{1,0:T(8,128)} fusion(bf16[384,3072]{1,0:T(8,128)(2,1)} %all-gather.3.cloned.1.call-done, bf16[3072,1024]{1,0:T(8,128)(2,1)} %param.12), kind=kOutput, calls=%fused_computation.50 | convolution fusion | flops 2415919104 | bytes 10223616 | tf_op jit(solution)/shard_map/dot_general | solution.py:45
  77.5 0.0 copy-done.2
  77.5 6.6 %fusion.32 = f32[384,1024]{1,0:T(8,128)} fusion(bf16[384,3072]{1,0:T(8,128)(2,1)S(1)} %copy-done.2, bf16[3072,1024]{1,0:T(8,128)(2,1)} %param.11), kind=kOutput, calls=%fused_computation.49 | convolution fusion | flops 2415919104 | bytes 10223616 | tf_op jit(solution)/shard_map/dot_general | solution.py:44
  84.1 44.5 %all-gather.5.cloned.1.call-done = bf16[384,3072]{1,0:T(8,128)(2,1)} async-done(((bf16[48,3072]{1,0:T(8,128)(2,1)}), bf16[384,3072]{1,0:T(8,128)(2,1)}) %all-gather.5.cloned.1.call-update) | async-done | bytes 2359312 | tf_op jit(solution)/shard_map/all_gather | solution.py:42
  128.6 0.0 slice-start
  128.6 8.5 %multiply_convert_fusion = (bf16[384,1024]{1,0:T(8,128)(2,1)S(1)}, bf16[384,1024]{1,0:T(8,128)(2,1)S(1)}, bf16[384,1024]{1,0:T(8,128)(2,1)}) fusion(f32[384,1024]{1,0:T(8,128)} %fusion.32, f32[384,1024]{1,0:T(8,128)} %fusion.33, bf16[384,3072]{1,0:T(8,128)(2,1)} %all-gather.5.cloned.1.call-done, bf16[1024,3072]{1,0:T(8,128)(2,1)} %param.13), kind=kOutput, calls=%fused_computation.10 | convolution fusion | flops 2421817344 | bytes 14155776 | tf_op jit(solution)/shard_map/dot_general | solution.py:28
  137.1 0.0 copy-start.3
  137.1 0.0 copy-start.4
  137.1 0.0 slice-start.1
  137.1 5.4 fusion.34
  142.5 0.0 copy-done.3
  142.5 0.0 copy-done.4
  142.5 0.0 slice-done
  142.5 0.0 slice-done.1
  142.5 4.0 add_convert_fusion
  146.6 0.0 reduce-scatter.8.cloned.1.call-update
  146.6 0.2 reduce-scatter.6.cloned.1.call-start
  146.8 7.0 %convolution_convert_fusion.3 = bf16[384,3072]{1,0:T(8,128)(2,1)} fusion(bf16[384,1024]{1,0:T(8,128)(2,1)} %get-tuple-element.7, bf16[1024,3072]{1,0:T(8,128)(2,1)} %param.13), kind=kOutput, calls=%fused_computation.4 | convolution fusion | flops 2417098752 | bytes 9437184 | tf_op jit(solution)/shard_map/dot_general | solution.py:54
  153.8 0.0 reduce-scatter.6.cloned.1.call-update
  153.9 0.0 reduce-scatter.14.cloned.1.call-start
  153.9 8.0 %convolution_convert_fusion = bf16[3072,1024]{1,0:T(8,128)(2,1)} fusion(bf16[384,3072]{1,0:T(8,128)(2,1)} %all-gather.5.cloned.1.call-done, bf16[384,1024]{1,0:T(8,128)(2,1)} %get-tuple-element.7), kind=kOutput, calls=%fused_computation | convolution fusion | flops 2419064832 | bytes 9437184 | tf_op jit(solution)/shard_map/dot_general | solution.py:22
  161.9 0.0 reduce-scatter.14.cloned.1.call-update
  161.9 0.0 reduce-scatter.12.cloned.1.call-start
  162.0 6.5 %convolution_convert_fusion.1 = bf16[3072,1024]{1,0:T(8,128)(2,1)} fusion(bf16[384,3072]{1,0:T(8,128)(2,1)S(1)} %copy-done.2, bf16[384,1024]{1,0:T(8,128)(2,1)} %copy-done.4), kind=kOutput, calls=%fused_computation.1 | convolution fusion | flops 2419064832 | bytes 9437184 | tf_op jit(solution)/shard_map/dot_general | solution.py:22
  168.5 0.0 reduce-scatter.12.cloned.1.call-update
  168.5 0.0 reduce-scatter.10.cloned.1.call-start
  168.6 6.5 %convolution_convert_fusion.2 = bf16[3072,1024]{1,0:T(8,128)(2,1)} fusion(bf16[384,3072]{1,0:T(8,128)(2,1)S(1)} %copy-done.2, bf16[384,1024]{1,0:T(8,128)(2,1)} %copy-done.3), kind=kOutput, calls=%fused_computation.2 | convolution fusion | flops 2419064832 | bytes 9437184 | tf_op jit(solution)/shard_map/dot_general | solution.py:22
  175.1 0.0 copy-start.1
  175.1 0.0 reduce-scatter.10.cloned.1.call-update
  175.1 47.2 %reduce-scatter.8.cloned.1.call-done = bf16[48,3072]{1,0:T(8,128)(2,1)} async-done(((bf16[384,3072]{1,0:T(8,128)(2,1)}), bf16[48,3072]{1,0:T(8,128)(2,1)}) %reduce-scatter.8.cloned.1.call-update) | async-done | bytes 294928 | tf_op jit(solution)/shard_map/reduce_scatter | solution.py:60
  222.3 2.7 convolution_convert_fusion.4
  225.0 77.3 %reduce-scatter.6.cloned.1.call-done = bf16[48,3072]{1,0:T(8,128)(2,1)} async-done(((bf16[384,3072]{1,0:T(8,128)(2,1)}), bf16[48,3072]{1,0:T(8,128)(2,1)}) %reduce-scatter.6.cloned.1.call-update) | async-done | bytes 294928 | tf_op jit(solution)/shard_map/reduce_scatter | solution.py:57
  302.3 0.0 copy-done.1
  302.3 2.7 fusion
  305.0 76.7 %reduce-scatter.14.cloned.1.call-done = bf16[192,1024]{1,0:T(8,128)(2,1)} async-done(((bf16[3072,1024]{1,0:T(8,128)(2,1)}), bf16[192,1024]{1,0:T(8,128)(2,1)}) %reduce-scatter.14.cloned.1.call-update) | async-done | bytes 393232 | tf_op jit(solution)/shard_map/reduce_scatter | solution.py:90
  381.6 79.7 %reduce-scatter.12.cloned.1.call-done = bf16[192,1024]{1,0:T(8,128)(2,1)} async-done(((bf16[3072,1024]{1,0:T(8,128)(2,1)}), bf16[192,1024]{1,0:T(8,128)(2,1)}) %reduce-scatter.12.cloned.1.call-update) | async-done | bytes 393232 | tf_op jit(solution)/shard_map/reduce_scatter | solution.py:87
  461.4 80.5 %reduce-scatter.10.cloned.1.call-done = bf16[192,1024]{1,0:T(8,128)(2,1)} async-done(((bf16[3072,1024]{1,0:T(8,128)(2,1)}), bf16[192,1024]{1,0:T(8,128)(2,1)}) %reduce-scatter.10.cloned.1.call-update) | async-done | bytes 393232 | tf_op jit(solution)/shard_map/reduce_scatter | solution.py:81
  (2 shorter events, 0.0 us)
Async XLA Ops:
  7.2 1.2 copy-start
  7.2 62.9 %all-gather.3.cloned.1.call-start = ((), (), s32[]{:S(2)}) async-start(), calls=%async_computation.5 | async-start | bytes 2654208 | tf_op jit(solution)/shard_map/all_gather | solution.py:41
  9.4 119.2 %all-gather.5.cloned.1.call-start = ((), (), s32[]{:S(2)}) async-start(), calls=%async_computation.7 | async-start | bytes 2654208 | tf_op jit(solution)/shard_map/all_gather | solution.py:42
  11.7 210.6 %reduce-scatter.8.cloned.1.call-start = ((), (), s32[]{:S(2)}) async-start(), calls=%async_computation.8 | async-start | bytes 2654208 | tf_op jit(solution)/shard_map/reduce_scatter | solution.py:60
  70.1 7.4 %copy-start.2 = (bf16[384,3072]{1,0:T(8,128)(2,1)S(1)}, bf16[384,3072]{1,0:T(8,128)(2,1)}, u32[]{:S(2)}) copy-start(bf16[384,3072]{1,0:T(8,128)(2,1)} %all-gather.3.cloned.1.call-done) | copy-start | bytes 7077892
  128.6 13.9 %slice-start = ((s8[6291456]{0:T(1024)(128)(4,1)}), s8[4194304]{0:T(1024)(128)(4,1)S(1)}, s32[]{:S(2)}) async-start(s8[6291456]{0:T(1024)(128)(4,1)} %bitcast.24), calls=%async_computation.12 | async-start | bytes 8388608
  137.1 5.4 copy-start.3
  137.1 5.4 copy-start.4
  137.1 5.4 slice-start.1
  146.6 155.7 %reduce-scatter.6.cloned.1.call-start = ((), (), s32[]{:S(2)}) async-start(), calls=%async_computation.6 | async-start | bytes 2654208 | tf_op jit(solution)/shard_map/reduce_scatter | solution.py:57
  153.9 227.8 %reduce-scatter.14.cloned.1.call-start = ((), (), s32[]{:S(2)}) async-start(), calls=%async_computation.11 | async-start | bytes 6684672 | tf_op jit(solution)/shard_map/reduce_scatter | solution.py:90
  161.9 299.4 %reduce-scatter.12.cloned.1.call-start = ((), (), s32[]{:S(2)}) async-start(), calls=%async_computation.10 | async-start | bytes 6684672 | tf_op jit(solution)/shard_map/reduce_scatter | solution.py:87
  168.5 373.3 %reduce-scatter.10.cloned.1.call-start = ((), (), s32[]{:S(2)}) async-start(), calls=%async_computation.9 | async-start | bytes 6684672 | tf_op jit(solution)/shard_map/reduce_scatter | solution.py:81
  175.1 127.2 %copy-start.1 = (f32[128]{0:T(128)S(1)}, f32[128]{0:T(128)}, u32[]{:S(2)}) copy-start(f32[128]{0:T(128)} %param.10) | copy-start | bytes 1540
Sparse Core Ops, SparseCore 0:
  10.9 59.1 all-gather.2
  73.0 55.5 all-gather.4
  146.7 75.5 reduce-scatter.7
  226.4 75.8 reduce-scatter.5
  305.1 76.4 reduce-scatter.13
  384.5 76.8 reduce-scatter.11
  464.3 77.4 reduce-scatter.9
where the time goes:
time: 549 us
  waiting for transfers between devices  464 us (85%)
  matrix products  68.4 us (12%)
  between operations  14.2 us (3%)
    reduce_scatter x1, waiting for transfers between devices, local(): lax.psum_scatter(contract_rows(rows_x, d_gate).astype(jnp.bfloat16), 'dp'...  80.5 us
    reduce_scatter x1, waiting for transfers between devices, local(): lax.psum_scatter(contract_rows(rows_x, d_up).astype(jnp.bfloat16), 'dp',...  79.7 us
    reduce_scatter x1, waiting for transfers between devices, local(): lax.psum_scatter(out_term.astype(jnp.bfloat16), 'tensor', scatter_dimensi...  77.3 us
    reduce_scatter x1, waiting for transfers between devices, local(): lax.psum_scatter(contract_rows(rows_d, hidden).astype(jnp.bfloat16), 'dp'...  76.7 us
    all_gather x1, waiting for transfers between devices, local(): lax.all_gather(x_sel, 'tensor', axis=0, tiled=True)  58.4 us
    reduce_scatter x1, waiting for transfers between devices, local(): lax.psum_scatter(back_term.astype(jnp.bfloat16), 'tensor', scatter_dimens...  47.2 us
    all_gather x1, waiting for transfers between devices, local(): lax.all_gather(d_sel, 'tensor', axis=0, tiled=True)  44.5 us
    dot_general x3, matrix products, contract_rows(): lax.dot_general(left_rows, right_rows, (((0,), (0,)), ((), ())), preferre...  21 us
  transfers between devices with their start and end apart: 7, of which 7 were waited for; matrix products, arithmetic and copies ran while one was open for 9% of the time, Pallas kernels for 0%

commit v1 on v0

v1 whole, which is shorter than its diff:
```python
import functools
import itertools

import jax
import jax.numpy as jnp
from jax import lax
from jax.experimental import pallas as pl
from jax.experimental.pallas import tpu as pltpu
from jax.sharding import PartitionSpec as P

SLOTS = 48
ROWS = 384
DW = 3072
FF = 1024
HALF = 512
FEAT = 384
BF = jnp.bfloat16
F32 = jnp.float32
VMEM = 56 * 1024 * 1024

DIM = (4, 2, 2, 2, 4)


def linear(place):
    r = 0
    for q, n in zip(place, DIM):
        r = r * n + q % n
    return r


def shift(value, axis, by):
    pairs = []
    for place in itertools.product(*map(range, DIM)):
        to = list(place)
        to[axis] += by
        pairs.append((linear(place), linear(to)))
    return lax.ppermute(value, ("dp", "tensor"), pairs)


to_x = lambda v, by: shift(v, 0, by)
to_zlo = lambda v: shift(v, 1, 1)
to_core = lambda v: shift(v, 2, 1)
to_zhi = lambda v: shift(v, 3, 1)
to_y = lambda v, by: shift(v, 4, by)


def dot(a, b):
    return jnp.dot(a, b, preferred_element_type=F32)


def dot_t(a, b):
    return lax.dot_general(a, b, (((1,), (1,)), ((), ())), preferred_element_type=F32)


def t_dot(a, b):
    return lax.dot_general(a, b, (((0,), (0,)), ((), ())), preferred_element_type=F32)


def cost(flops, nbytes):
    return pl.CostEstimate(flops=int(flops), bytes_accessed=int(nbytes), transcendentals=0)


def params():
    return pltpu.CompilerParams(vmem_limit_bytes=VMEM)


def picks_of(ids, weight):
    n = ids.shape[1]
    chosen = (ids[0:1] == 0) | (ids[1:2] == 0)
    ones = jnp.where(chosen, 1.0, 0.0).astype(BF)
    before = lax.broadcasted_iota(jnp.int32, (n, n), 0) <= lax.broadcasted_iota(jnp.int32, (n, n), 1)
    place = dot(jnp.broadcast_to(ones, (8, n)), jnp.where(before, 1.0, 0.0).astype(BF))[0:1]
    place = place.astype(jnp.int32) - 1
    slot = lax.broadcasted_iota(jnp.int32, (SLOTS, n), 0)
    picks = jnp.where((place == slot) & chosen, 1.0, 0.0)
    return picks.astype(BF), jnp.sum(picks * weight, axis=1, keepdims=True)


def select_kernel(ids, weight, tokens, cotangent, x_sel, d_sel):
    picks, slot_weight = picks_of(ids[...], weight[...])
    x_sel[...] = dot(picks, tokens[...]).astype(BF)
    d_sel[...] = (dot(picks, cotangent[...]) * slot_weight).astype(BF)


def select(ids, weight, tokens, cotangent):
    out = jax.ShapeDtypeStruct((SLOTS, DW), BF)
    return pl.pallas_call(
        select_kernel,
        out_shape=(out, out),
        compiler_params=params(),
        cost_estimate=cost(4 * SLOTS * 128 * DW, 2.2e6),
    )(ids, weight, tokens, cotangent)


def place_kernel(scaled, ids, weight, own, got, out):
    picks, slot_weight = picks_of(ids[...], weight[...])
    total = own[...].astype(F32) + got[...].astype(F32)
    if scaled:
        total = total * slot_weight
    out[...] = t_dot(picks, total.astype(BF)).astype(BF)


def place(scaled, ids, weight, own, got):
    return pl.pallas_call(
        functools.partial(place_kernel, scaled),
        out_shape=jax.ShapeDtypeStruct((128, DW), BF),
        compiler_params=params(),
        cost_estimate=cost(2 * SLOTS * 128 * DW, 1.4e6),
    )(ids, weight, own, got)


def column(j, core):
    return ((1 - core[0]) * 2 + j) % 4


def chunk_spec():
    return pl.BlockSpec((SLOTS, DW), lambda j, core: (0, 0))


def natural_spec():
    return pl.BlockSpec((ROWS, 256), lambda j, core: (0, column(j, core)))


def sent_spec():
    return pl.BlockSpec((ROWS, 256), lambda j, core: (0, jnp.minimum(j, 1)))


def gate_kernel(core, *refs):
    chunks, (w_gate, w_up, rows, hidden, sent, act, slope) = refs[:8], refs[8:]
    j = pl.program_id(0)

    @pl.when(j == 0)
    def _():
        for k in range(8):
            rows[k * SLOTS : (k + 1) * SLOTS] = chunks[k][...]

    x = rows[...]
    gate = dot(x, w_gate[...])
    up = dot(x, w_up[...])
    s = jax.nn.sigmoid(gate)
    silu = gate * s
    act[...] = silu
    slope[...] = up * s * (1.0 + gate * (1.0 - s))
    h = (silu * up).astype(BF)
    hidden[...] = h

    @pl.when(j < 2)
    def _():
        sent[...] = h


def gate_up(core, chunks, w_gate, w_up):
    weight = pl.BlockSpec((DW, 256), lambda j, core: (0, column(j, core)))
    return pl.pallas_call(
        gate_kernel,
        grid_spec=pltpu.PrefetchScalarGridSpec(
            num_scalar_prefetch=1,
            grid=(4,),
            in_specs=[chunk_spec()] * 8 + [weight, weight],
            out_specs=[
                pl.BlockSpec((ROWS, DW), lambda j, core: (0, 0)),
                natural_spec(),
                sent_spec(),
                natural_spec(),
                natural_spec(),
            ],
        ),
        out_shape=(
            jax.ShapeDtypeStruct((ROWS, DW), BF),
            jax.ShapeDtypeStruct((ROWS, FF), BF),
            jax.ShapeDtypeStruct((ROWS, HALF), BF),
            jax.ShapeDtypeStruct((ROWS, FF), F32),
            jax.ShapeDtypeStruct((ROWS, FF), F32),
        ),
        compiler_params=params(),
        cost_estimate=cost(4 * ROWS * DW * FF, 21e6),
    )(core, *chunks, w_gate, w_up)


def back_kernel(core, *refs):
    chunks, (w_down, act, slope, rows, d_gate, d_up, sent) = refs[:8], refs[8:]
    j = pl.program_id(0)

    @pl.when(j == 0)
    def _():
        for k in range(8):
            rows[k * SLOTS : (k + 1) * SLOTS] = chunks[k][...]

    d_hidden = dot_t(rows[...], w_down[...])
    du = (d_hidden * act[...]).astype(BF)
    dg = (d_hidden * slope[...]).astype(BF)
    d_up[...] = du
    d_gate[...] = dg

    @pl.when(j < 2)
    def _():
        sent[0] = dg
        sent[1] = du


def back_hidden(core, chunks, w_down, act, slope):
    return pl.pallas_call(
        back_kernel,
        grid_spec=pltpu.PrefetchScalarGridSpec(
            num_scalar_prefetch=1,
            grid=(4,),
            in_specs=[chunk_spec()] * 8
            + [
                pl.BlockSpec((256, DW), lambda j, core: (column(j, core), 0)),
                natural_spec(),
                natural_spec(),
            ],
            out_specs=[
                pl.BlockSpec((ROWS, DW), lambda j, core: (0, 0)),
                natural_spec(),
                natural_spec(),
                pl.BlockSpec((2, ROWS, 256), lambda j, core: (0, 0, jnp.minimum(j, 1))),
            ],
        ),
        out_shape=(
            jax.ShapeDtypeStruct((ROWS, DW), BF),
            jax.ShapeDtypeStruct((ROWS, FF), BF),
            jax.ShapeDtypeStruct((ROWS, FF), BF),
            jax.ShapeDtypeStruct((2, ROWS, HALF), BF),
        ),
        compiler_params=params(),
        cost_estimate=cost(2 * ROWS * DW * FF, 16e6),
    )(core, *chunks, w_down, act, slope)


def out_kernel(hidden, w_down, out):
    out[...] = dot(hidden[...], w_down[...]).astype(BF)


def out_terms(hidden, w_down):
    return pl.pallas_call(
        out_kernel,
        grid=(4,),
        in_specs=[
            pl.BlockSpec((ROWS, FF), lambda j: (0, 0)),
            pl.BlockSpec((FF, 768), lambda j: (0, j)),
        ],
        out_specs=pl.BlockSpec((ROWS, 768), lambda j: (0, j)),
        out_shape=jax.ShapeDtypeStruct((ROWS, DW), BF),
        compiler_params=params(),
        cost_estimate=cost(2 * ROWS * DW * FF, 10e6),
    )(hidden, w_down)


def token_kernel(d_gate, d_up, w_gate, w_up, out):
    out[...] = (dot_t(d_gate[...], w_gate[...]) + dot_t(d_up[...], w_up[...])).astype(BF)


def token_terms(d_gate, d_up, w_gate, w_up):
    rows = pl.BlockSpec((ROWS, FF), lambda j: (0, 0))
    weight = pl.BlockSpec((768, FF), lambda j: (j, 0))
    return pl.pallas_call(
        token_kernel,
        grid=(4,),
        in_specs=[rows, rows, weight, weight],
        out_specs=pl.BlockSpec((ROWS, 768), lambda j: (0, j)),
        out_shape=jax.ShapeDtypeStruct((ROWS, DW), BF),
        compiler_params=params(),
        cost_estimate=cost(4 * ROWS * DW * FF, 18e6),
    )(d_gate, d_up, w_gate, w_up)


def both(own, other):
    return jnp.concatenate([own[...], other[...]], axis=0)


def feature_spec():
    return pl.BlockSpec((ROWS, FEAT), lambda j, core, order: (0, order[j]))


def half_spec():
    return pl.BlockSpec((ROWS, HALF), lambda j, core, order: (0, core[0]))


def other_spec():
    return pl.BlockSpec((ROWS, HALF), lambda j, core, order: (0, 0))


def grads_kernel(core, order, x_own, x_other, g_own, g_other, u_own, u_other, gate, up):
    x = both(x_own, x_other)
    gate[0] = t_dot(x, both(g_own, g_other)).astype(BF)
    up[0] = t_dot(x, both(u_own, u_other)).astype(BF)


def gate_up_grads(core, order, x_own, x_other, d_gate, d_up, got):
    g_other = pl.BlockSpec((None, ROWS, HALF), lambda j, core, order: (0, 0, 0))
    u_other = pl.BlockSpec((None, ROWS, HALF), lambda j, core, order: (1, 0, 0))
    out = pl.BlockSpec((1, FEAT, HALF), lambda j, core, order: (j, 0, 0))
    shape = jax.ShapeDtypeStruct((8, FEAT, HALF), BF)
    return pl.pallas_call(
        grads_kernel,
        grid_spec=pltpu.PrefetchScalarGridSpec(
            num_scalar_prefetch=2,
            grid=(8,),
            in_specs=[
                feature_spec(),
                feature_spec(),
                half_spec(),
                g_other,
                half_spec(),
                u_other,
            ],
            out_specs=[out, out],
        ),
        out_shape=(shape, shape),
        compiler_params=params(),
        cost_estimate=cost(4 * ROWS * DW * FF, 13e6),
    )(core, order, x_own, x_other, d_gate, got, d_up, got)


def down_kernel(core, order, d_own, d_other, h_own, h_other, out, h_turned):
    @pl.when(pl.program_id(0) == 0)
    def _():
        h_turned[...] = both(h_own, h_other).T

    out[0] = dot(h_turned[...], both(d_own, d_other)).astype(BF)


def down_grads(core, order, d_own, d_other, hidden, got):
    return pl.pallas_call(
        down_kernel,
        grid_spec=pltpu.PrefetchScalarGridSpec(
            num_scalar_prefetch=2,
            grid=(8,),
            in_specs=[feature_spec(), feature_spec(), half_spec(), other_spec()],
            out_specs=pl.BlockSpec((1, HALF, FEAT), lambda j, core, order: (j, 0, 0)),
            scratch_shapes=[pltpu.VMEM((HALF, 2 * ROWS), BF)],
        ),
        out_shape=jax.ShapeDtypeStruct((8, HALF, FEAT), BF),
        compiler_params=params(),
        cost_estimate=cost(2 * ROWS * DW * FF, 9e6),
    )(core, order, d_own, d_other, hidden, got)


def add(*terms):
    return sum(t.astype(F32) for t in terms).astype(BF)


def gather_rows(own):
    up0 = to_y(own, -1)
    down0 = to_y(own, 1)
    other = to_zhi(own)
    far0 = to_y(up0, -1)
    up1 = to_y(other, -1)
    down1 = to_y(other, 1)
    far1 = to_y(down1, 1)
    return [far0, far1, up0, up1, down0, down1, own, other]


def sum_rows(terms):
    t = [terms[k * SLOTS : (k + 1) * SLOTS] for k in range(8)]
    a = to_y(t[0], 1)
    b = to_y(t[1], -1)
    above = to_y(jnp.concatenate([add(t[2], a), t[3]], axis=0), 1)
    below = to_y(jnp.concatenate([t[4], add(t[5], b)], axis=0), -1)
    own = add(t[6], above[:SLOTS], below[:SLOTS])
    other = add(t[7], above[SLOTS:], below[SLOTS:])
    return own, to_zhi(other)


def sum_x(far, far_other, near, back, own):
    a = to_x(far, 1)
    b = to_x(far_other, -1)
    above = to_x(jnp.concatenate([add(near[0], a), near[1]], axis=0), 1)
    below = to_x(jnp.concatenate([back[0], add(back[1], b)], axis=0), -1)
    return add(own, above, below)


def sum_x_first(m):
    s = sum_x(m[0:1], m[1:2], (m[2:3], m[3:4]), (m[4:5], m[5:6]), m[6:8])
    return add(s[0], to_zlo(s[1]))


def sum_zlo_first(m):
    got = to_zlo(m[0:4])
    s = add(m[4:8], got)
    h = s.shape[1] // 2
    parts = lambda k: (s[k, :h], s[k, h:])
    return sum_x(*parts(0), parts(1), parts(2), s[3])


def local(tokens, cotangent, expert_ids, combine, w_gate, w_up, w_down):
    dp = lax.axis_index("dp")
    x, zlo, c = dp // 4, (dp // 2) % 2, dp % 2
    core = c.astype(jnp.int32).reshape(1)

    def order_of(steps):
        return jnp.stack([((x + dx) % 4) * 2 + (zlo + dz) % 2 for dx, dz in steps]).astype(jnp.int32)

    x_first = order_of([(dx, dz) for dx in (2, 1, 3, 0) for dz in (0, 1)])
    ids, weight = expert_ids.T, combine.reshape(1, -1)

    x_sel, d_sel = select(ids, weight, tokens, cotangent)
    x_chunks = gather_rows(x_sel)
    d_chunks = gather_rows(d_sel)
    x_rows, hidden, hidden_sent, act, slope = gate_up(core, x_chunks, w_gate, w_up)
    x_other = to_core(x_rows)
    hidden_got = to_core(hidden_sent)
    out = out_terms(hidden, w_down)
    d_rows, d_gate, d_up, d_sent = back_hidden(core, d_chunks, w_down, act, slope)
    d_got = to_core(d_sent)
    d_other = to_core(d_rows)
    gate, up = gate_up_grads(core, x_first, x_rows, x_other, d_gate, d_up, d_got)
    zlo_first = order_of([(dx, dz) for dz in (1, 0) for dx in (2, 1, 3, 0)])
    down = down_grads(core, zlo_first, d_rows, d_other, hidden, hidden_got)
    back = token_terms(d_gate, d_up, w_gate, w_up)

    gate_sum = sum_x_first(gate)
    up_sum = sum_x_first(up)
    down_sum = sum_zlo_first(down)
    out_own, out_got = sum_rows(out)
    back_own, back_got = sum_rows(back)
    expert_output = place(True, ids, weight, out_own, out_got)
    token_grad = place(False, ids, weight, back_own, back_got)

    def join(s, axis, other_axis):
        low, high = jnp.split(s, 2, axis=axis)
        keep = jnp.where(c == 0, low, high)
        got = to_core(jnp.where(c == 0, high, low))
        first, second = jnp.where(c == 0, keep, got), jnp.where(c == 0, got, keep)
        return jnp.concatenate([first, second], axis=other_axis)

    return (expert_output, token_grad, join(gate_sum, 0, 1), join(up_sum, 0, 1), join(down_sum, 1, 0))


def solution(mesh):
    placed = (
        P(("dp", "tensor"), None),
        P(("dp", "tensor"), None),
        P(("dp", "tensor"), None),
        P(("dp", "tensor")),
        P(None, "tensor"),
        P(None, "tensor"),
        P("tensor", None),
    )
    return jax.shard_map(
        local,
        mesh=mesh,
        in_specs=placed,
        out_specs=(
            P(("dp", "tensor"), None),
            P(("dp", "tensor"), None),
            P("dp", "tensor"),
            P("dp", "tensor"),
            P("tensor", "dp"),
        ),
        check_vma=False,
    )
```

time: 549 us -> 244 us (0.44)
  waiting for transfers between devices: 464 us -> 74.5 us
  starting transfers between devices: 0.47 us -> 72.7 us
  matrix products: 68.4 us -> 0 us
  Pallas kernels: 0 us -> 65 us
  other arithmetic: 1.04 us -> 18.8 us
  between operations: 14.2 us -> 1.06 us
  local copies, waits for them, and re-layouts: 0.15 us -> 11 us
    reduce_scatter x5 -> x0, waiting for transfers between devices: 361 us -> none  [the longest x1 80.5 us: local(): lax.psum_scatter(contract_rows(rows_x, d_gate).astype(jnp.bfloat16), 'dp'...]
    all_gather x2 -> x0, waiting for transfers between devices: 103 us -> none  [the longest x1 58.4 us: local(): lax.all_gather(x_sel, 'tensor', axis=0, tiled=True)]
    ppermute x0 -> x46, waiting for transfers between devices: none -> 74.5 us  [shift(): return lax.ppermute(value, ('dp', 'tensor'), pairs)]
    ppermute x0 -> x46, starting transfers between devices: none -> 72.7 us  [shift(): return lax.ppermute(value, ('dp', 'tensor'), pairs)]
    dot_general x13 -> x0, matrix products: 68.4 us -> none  [the longest x3 21 us: contract_rows(): lax.dot_general(left_rows, right_rows, (((0,), (0,)), ((), ())), preferre...]
    pallas_call x0 -> x9, Pallas kernels: none -> 65 us  [the longest x1 11.5 us: gate_up(): pl.pallas_call(gate_kernel, grid_spec=pltpu.PrefetchScalarGridSpec(num_sc...]
    convert_element_type x1 -> x13, other arithmetic: 0.01 us -> 11 us  [add(): return sum((t.astype(F32) for t in terms)).astype(BF)]
    concatenate x0 -> x13, other arithmetic: none -> 7.4 us  [the longest x3 1.99 us: sum_x(): below = to_x(jnp.concatenate([back[0], add(back[1], b)], axis=0), -1)]
  transfers between devices with their start and end apart: 7 -> 46, of which waited for: 7 -> 16; matrix products, arithmetic and copies ran while one was open for 9% -> 11% of each run, Pallas kernels for 0% -> 22%
where the time goes in v1:
time: 244 us; the launch traced here: 243 us
  waiting for transfers between devices  74.5 us (31%)
  starting transfers between devices  72.7 us (30%)
  Pallas kernels  65 us (27%)
  other arithmetic  18.8 us (8%)
  local copies, waits for them, and re-layouts  11 us (5%)
    ppermute x46, waiting for transfers between devices, shift(): return lax.ppermute(value, ('dp', 'tensor'), pairs)  74.5 us
    ppermute x46, starting transfers between devices, shift(): return lax.ppermute(value, ('dp', 'tensor'), pairs)  72.7 us
    pallas_call x1, Pallas kernels, gate_up(): pl.pallas_call(gate_kernel, grid_spec=pltpu.PrefetchScalarGridSpec(num_sc...  11.5 us
    convert_element_type x13, other arithmetic, add(): return sum((t.astype(F32) for t in terms)).astype(BF)  11 us
    pallas_call x1, Pallas kernels, gate_up_grads(): pl.pallas_call(grads_kernel, grid_spec=pltpu.PrefetchScalarGridSpec(num_s...  10.8 us
    pallas_call x1, Pallas kernels, token_terms(): pl.pallas_call(token_kernel, grid=(4,), in_specs=[rows, rows, weight, wei...  9.74 us
    pallas_call x1, Pallas kernels, down_grads(): pl.pallas_call(down_kernel, grid_spec=pltpu.PrefetchScalarGridSpec(num_sc...  9.67 us
    pallas_call x1, Pallas kernels, back_hidden(): pl.pallas_call(back_kernel, grid_spec=pltpu.PrefetchScalarGridSpec(num_sc...  9.03 us
  transfers between devices with their start and end apart: 46, of which 16 were waited for; matrix products, arithmetic and copies ran while one was open for 11% of the time, Pallas kernels for 22%

profile of v1, /device:TPU:1, one launch (start us, length us, event | category | flops | bytes accessed | tf_op | source)
XLA Modules:
  0.0 243.0 jit_solution(15378214649267365875)
XLA Ops:
  0.6 2.6 %shard_map.110 = (bf16[48,3072]{1,0:T(8,128)(2,1)}, bf16[48,3072]{1,0:T(8,128)(2,1)}) custom-call(s32[2,128]{1,0:T(2,128)} %bitcast.48, f32[1,128]{1,0:T(1,128)} %bitcast.51, bf16[128,3072]{1,0:T(8,128)(2,1)} %tokens.1, bf16[128,3072]{1,0:T(8,128)(2,1)} %cotangent.1), custom_call_target="tpu_custom_call" | custom-call | flops 75497472 | bytes 2200000 | tf_op jit(solution)/shard_map/pallas_call | solution.py:87
  3.2 4.4 %collective-permute-start.2 = (bf16[48,3072]{1,0:T(8,128)(2,1)}, bf16[48,3072]{1,0:T(8,128)(2,1)S(1)}, u32[]{:S(2)}, u32[]{:S(2)}) collective-permute-start(bf16[48,3072]{1,0:T(8,128)(2,1)} %get-tuple-element.18.refs_6_), channel_id=1, source_target_pairs={{0,4},{1,5},{2,6},{3,7},{4,0},{5,1},{6,2},{7,3},{8,12},{9,13},{10,... | collective-permute-start | bytes 884744 | tf_op jit(solution)/shard_map/ppermute | solution.py:37
  7.7 2.7 %collective-permute-start = (bf16[48,3072]{1,0:T(8,128)(2,1)}, bf16[48,3072]{1,0:T(8,128)(2,1)S(1)}, u32[]{:S(2)}, u32[]{:S(2)}) collective-permute-start(bf16[48,3072]{1,0:T(8,128)(2,1)} %get-tuple-element.18.refs_6_), channel_id=1, source_target_pairs={{0,3},{1,0},{2,1},{3,2},{4,7},{5,4},{6,5},{7,6},{8,11},{9,8},{10,9... | collective-permute-start | bytes 884744 | tf_op jit(solution)/shard_map/ppermute | solution.py:37
  10.4 4.2 %collective-permute-done.2.refs_7_ = bf16[48,3072]{1,0:T(8,128)(2,1)S(1)} collective-permute-done((bf16[48,3072]{1,0:T(8,128)(2,1)}, bf16[48,3072]{1,0:T(8,128)(2,1)S(1)}, u32[]{:S(2)}, u32[]{:S(2)}) %collective-permute-start.2) | collective-permute-done | bytes 294944 | tf_op jit(solution)/shard_map/ppermute | solution.py:37
  14.6 1.3 collective-permute-start.3
  15.9 1.4 collective-permute-start.12
  17.4 2.0 collective-permute-start.5
  19.5 1.1 collective-permute-done.14.refs_7_
  20.6 1.6 collective-permute-start.15
  22.2 3.2 %collective-permute-done.3.refs_5_ = bf16[48,3072]{1,0:T(8,128)(2,1)S(1)} collective-permute-done((bf16[48,3072]{1,0:T(8,128)(2,1)S(1)}, bf16[48,3072]{1,0:T(8,128)(2,1)S(1)}, u32[]{:S(2)}, u32[]{:S(2)}) %collective-permute-start.3) | collective-permute-done | bytes 294944 | tf_op jit(solution)/shard_map/ppermute | solution.py:37
  26.6 2.0 collective-permute-done.5.refs_3_
  28.6 3.0 %collective-permute-start.17 = (bf16[48,3072]{1,0:T(8,128)(2,1)S(1)}, bf16[48,3072]{1,0:T(8,128)(2,1)S(1)}, u32[]{:S(2)}, u32[]{:S(2)}) collective-permute-start(bf16[48,3072]{1,0:T(8,128)(2,1)S(1)} %collective-permute-done.14.refs_7_), channel_id=1, source_target_pairs={{0,3},{1,0},{2,1},{3,2},{4,7},{5,4},{6,5},{7,6},{8,11},{9,8},{10,9... | collective-permute-start | bytes 884744 | tf_op jit(solution)/shard_map/ppermute | solution.py:37
  31.6 3.3 %collective-permute-done.1.refs_0_ = bf16[48,3072]{1,0:T(8,128)(2,1)S(1)} collective-permute-done((bf16[48,3072]{1,0:T(8,128)(2,1)S(1)}, bf16[48,3072]{1,0:T(8,128)(2,1)S(1)}, u32[]{:S(2)}, u32[]{:S(2)}) %collective-permute-start.1) | collective-permute-done | bytes 294944 | tf_op jit(solution)/shard_map/ppermute | solution.py:37
  34.9 3.0 %collective-permute-start.13 = (bf16[48,3072]{1,0:T(8,128)(2,1)S(1)}, bf16[48,3072]{1,0:T(8,128)(2,1)S(1)}, u32[]{:S(2)}, u32[]{:S(2)}) collective-permute-start(bf16[48,3072]{1,0:T(8,128)(2,1)S(1)} %collective-permute-done.12.refs_2_), channel_id=1, source_target_pairs={{0,3},{1,0},{2,1},{3,2},{4,7},{5,4},{6,5},{7,6},{8,11},{9,8},{10,9... | collective-permute-start | bytes 884744 | tf_op jit(solution)/shard_map/ppermute | solution.py:37
  38.8 11.5 %shard_map.111 = (bf16[384,3072]{1,0:T(8,128)(2,1)}, bf16[384,1024]{1,0:T(8,128)(2,1)}, bf16[384,512]{1,0:T(8,128)(2,1)}, f32[384,1024]{1,0:T(8,128)}, f32[384,1024]{1,0:T(8,128)}) custom-call(s32[1]{0:T(128)} %bitcast.2.core, bf16[48,3072]{1,0:T(8,128)(2,1)} %copy-done.21, bf16[48,3072]{1,0:T(8,128)(2,1)} %copy-done.22, bf16[48,3072]{1,0:T(8,128)(2,1)} %copy-done.17, ...), custom_call_target="tpu_custom_call" | custom-call | flops 4831838208 | bytes 21000000 | tf_op jit(solution)/shard_map/pallas_call | solution.py:154
  51.3 9.0 %shard_map.114 = (bf16[384,3072]{1,0:T(8,128)(2,1)}, bf16[384,1024]{1,0:T(8,128)(2,1)}, bf16[384,1024]{1,0:T(8,128)(2,1)}, bf16[2,384,512]{2,1,0:T(8,128)(2,1)}) custom-call(s32[1]{0:T(128)} %bitcast.2.core, bf16[48,3072]{1,0:T(8,128)(2,1)} %copy-done.12, bf16[48,3072]{1,0:T(8,128)(2,1)} %copy-done.13, bf16[48,3072]{1,0:T(8,128)(2,1)} %copy-done.7, ...), custom_call_target="tpu_custom_call" | custom-call | flops 2415919104 | bytes 16000000 | tf_op jit(solution)/shard_map/pallas_call | solution.py:202
  60.3 5.7 %collective-permute-start.38 = (bf16[384,3072]{1,0:T(8,128)(2,1)}, bf16[384,3072]{1,0:T(8,128)(2,1)S(1)}, u32[]{:S(2)}, u32[]{:S(2)}) collective-permute-start(bf16[384,3072]{1,0:T(8,128)(2,1)} %get-tuple-element.29.d_own), channel_id=1, source_target_pairs={{0,8},{1,9},{2,10},{3,11},{4,12},{5,13},{6,14},{7,15},{8,0},{9,1},... | collective-permute-start | bytes 7077896 | tf_op jit(solution)/shard_map/ppermute | solution.py:37
  66.5 9.7 %shard_map.115 = bf16[384,3072]{1,0:T(8,128)(2,1)} custom-call(bf16[384,1024]{1,0:T(8,128)(2,1)} %get-tuple-element.23.d_gate.g_own, bf16[384,1024]{1,0:T(8,128)(2,1)} %get-tuple-element.24.d_up.u_own, bf16[3072,1024]{1,0:T(8,128)(2,1)} %w_gate.1, bf16[3072,1024]{1,0:T(8,128)(2,1)} %w_up.1), custom_call_target="tpu_custom_call" | custom-call | flops 4831838208 | bytes 18000000 | tf_op jit(solution)/shard_map/pallas_call | solution.py:257
  76.2 1.3 fusion.8
  78.3 2.3 collective-permute-start.21
  80.6 6.6 %shard_map.112 = bf16[384,3072]{1,0:T(8,128)(2,1)} custom-call(bf16[384,1024]{1,0:T(8,128)(2,1)} %get-tuple-element.19.hidden.h_own, bf16[1024,3072]{1,0:T(8,128)(2,1)} %refs_8_.3), custom_call_target="tpu_custom_call" | custom-call | flops 2415919104 | bytes 10000000 | tf_op jit(solution)/shard_map/pallas_call | solution.py:236
  87.3 1.5 fusion.9
  88.8 2.7 %collective-permute-start.9 = (bf16[48,3072]{1,0:T(8,128)(2,1)S(1)}, bf16[48,3072]{1,0:T(8,128)(2,1)S(1)}, u32[]{:S(2)}, u32[]{:S(2)}) collective-permute-start(bf16[48,3072]{1,0:T(8,128)(2,1)S(1)} %get-tuple-element.61), channel_id=1, source_target_pairs={{0,3},{1,0},{2,1},{3,2},{4,7},{5,4},{6,5},{7,6},{8,11},{9,8},{10,9... | collective-permute-start | bytes 884744 | tf_op jit(solution)/shard_map/ppermute | solution.py:37
  91.7 6.5 %collective-permute-done.7 = bf16[48,3072]{1,0:T(8,128)(2,1)S(1)} collective-permute-done((bf16[48,3072]{1,0:T(8,128)(2,1)S(1)}, bf16[48,3072]{1,0:T(8,128)(2,1)S(1)}, u32[]{:S(2)}, u32[]{:S(2)}) %collective-permute-start.7) | collective-permute-done | bytes 294944 | tf_op jit(solution)/shard_map/ppermute | solution.py:37
  98.3 2.7 %collective-permute-start.22 = (bf16[96,3072]{1,0:T(8,128)(2,1)S(1)}, bf16[96,3072]{1,0:T(8,128)(2,1)S(1)}, u32[]{:S(2)}, u32[]{:S(2)}) collective-permute-start(bf16[96,3072]{1,0:T(8,128)(2,1)S(1)} %pad_maximum_fusion.7), channel_id=1, source_target_pairs={{0,3},{1,0},{2,1},{3,2},{4,7},{5,4},{6,5},{7,6},{8,11},{9,8},{10,9... | collective-permute-start | bytes 1769480 | tf_op jit(solution)/shard_map/ppermute | solution.py:37
  102.8 10.3 %collective-permute-done.20 = bf16[96,3072]{1,0:T(8,128)(2,1)S(1)} collective-permute-done((bf16[96,3072]{1,0:T(8,128)(2,1)S(1)}, bf16[96,3072]{1,0:T(8,128)(2,1)S(1)}, u32[]{:S(2)}, u32[]{:S(2)}) %collective-permute-start.20) | collective-permute-done | bytes 589856 | tf_op jit(solution)/shard_map/ppermute | solution.py:37
  113.1 2.1 collective-permute-start.39
  115.2 1.0 add_convert_fusion.7
  116.2 2.7 %collective-permute-start.10 = (bf16[96,3072]{1,0:T(8,128)(2,1)}, bf16[96,3072]{1,0:T(8,128)(2,1)}, u32[]{:S(2)}, u32[]{:S(2)}) collective-permute-start(bf16[96,3072]{1,0:T(8,128)(2,1)} %pad_maximum_fusion.5), channel_id=1, source_target_pairs={{0,3},{1,0},{2,1},{3,2},{4,7},{5,4},{6,5},{7,6},{8,11},{9,8},{10,9... | collective-permute-start | bytes 1769480 | tf_op jit(solution)/shard_map/ppermute | solution.py:37
  118.9 3.5 %collective-permute-start.23 = (bf16[48,3072]{1,0:T(8,128)(2,1)}, bf16[48,3072]{1,0:T(8,128)(2,1)}, u32[]{:S(2)}, u32[]{:S(2)}) collective-permute-start(bf16[48,3072]{1,0:T(8,128)(2,1)} %get-tuple-element.36), channel_id=1, source_target_pairs={{0,4},{1,5},{2,6},{3,7},{4,0},{5,1},{6,2},{7,3},{8,12},{9,13},{10,... | collective-permute-start | bytes 884744 | tf_op jit(solution)/shard_map/ppermute | solution.py:37
  122.5 10.8 %shard_map.117 = (bf16[8,384,512]{2,1,0:T(8,128)(2,1)}, bf16[8,384,512]{2,1,0:T(8,128)(2,1)}) custom-call(s32[1]{0:T(128)} %bitcast.2.core, s32[8]{0:T(128)} %stack.46.order, bf16[384,3072]{1,0:T(8,128)(2,1)} %get-tuple-element.25.x_own, bf16[384,3072]{1,0:T(8,128)(2,1)} %collective-permute-done.24.x_other, ...), custom_call_target="tpu_custom_call" | custom-call | flops 4831838208 | bytes 13000000 | tf_op jit(solution)/shard_map/pallas_call | solution.py:295
  133.3 1.6 fusion.6
  134.9 1.3 collective-permute-start.32
  136.2 1.5 collective-permute-start.34
  137.7 2.3 add_convert_fusion.11
  140.0 6.0 %collective-permute-done.32 = bf16[1,384,512]{2,1,0:T(8,128)(2,1)S(1)} collective-permute-done((bf16[1,384,512]{2,1,0:T(8,128)(2,1)S(1)}, bf16[1,384,512]{2,1,0:T(8,128)(2,1)S(1)}, u32[]{:S(2)}, u32[]{:S(2)}) %collective-permute-start.32) | collective-permute-done | bytes 393248 | tf_op jit(solution)/shard_map/ppermute | solution.py:37
  146.0 2.7 %collective-permute-start.28 = (bf16[1,384,512]{2,1,0:T(8,128)(2,1)S(1)}, bf16[1,384,512]{2,1,0:T(8,128)(2,1)S(1)}, u32[]{:S(2)}, u32[]{:S(2)}) collective-permute-start(bf16[1,384,512]{2,1,0:T(8,128)(2,1)S(1)} %get-tuple-element.49), channel_id=1, source_target_pairs={{0,96},{1,97},{2,98},{3,99},{4,100},{5,101},{6,102},{7,103},{8,104... | collective-permute-start | bytes 1179656 | tf_op jit(solution)/shard_map/ppermute | solution.py:37
  148.7 1.3 add_convert_fusion.4
  150.0 0.9 pad_maximum_fusion.2
  151.0 1.0 pad_maximum_fusion.3
  152.0 2.7 %collective-permute-start.35 = (bf16[2,384,512]{2,1,0:T(8,128)(2,1)}, bf16[2,384,512]{2,1,0:T(8,128)(2,1)}, u32[]{:S(2)}, u32[]{:S(2)}) collective-permute-start(bf16[2,384,512]{2,1,0:T(8,128)(2,1)} %pad_maximum_fusion.3), channel_id=1, source_target_pairs={{0,96},{1,97},{2,98},{3,99},{4,100},{5,101},{6,102},{7,103},{8,104... | collective-permute-start | bytes 2359304 | tf_op jit(solution)/shard_map/ppermute | solution.py:37
  154.6 9.7 %shard_map.118 = bf16[8,512,384]{2,1,0:T(8,128)(2,1)} custom-call(s32[1]{0:T(128)} %bitcast.2.core, s32[8]{0:T(128)} %stack.47.order, bf16[384,3072]{1,0:T(8,128)(2,1)} %get-tuple-element.29.d_own, bf16[384,3072]{1,0:T(8,128)(2,1)} %copy-done.3, bf16[384,1024]{1,0:T(8,128)(2,1)} %get-tuple-element.19.hidden.h_own, bf16[384,512]{1,0:T(8,128)(2,1)} %copy-done.5), custom_call_target="tpu_custom_call" | custom-call | flops 2415919104 | bytes 9000000 | tf_op jit(solution)/shard_map/pallas_call | solution.py:325
  164.3 2.8 %slice.233 = bf16[4,512,384]{2,1,0:T(8,128)(2,1)} slice(bf16[8,512,384]{2,1,0:T(8,128)(2,1)} %shard_map.118), slice={[0:4], [0:512], [0:384]} | slice | bytes 3145728 | tf_op jit(solution)/shard_map/slice | solution.py:380
  168.4 0.9 pad_maximum_fusion
  169.3 1.0 pad_maximum_fusion.1
  170.3 3.9 %collective-permute-done.11.got = bf16[48,3072]{1,0:T(8,128)(2,1)S(1)} collective-permute-done((bf16[48,3072]{1,0:T(8,128)(2,1)S(1)}, bf16[48,3072]{1,0:T(8,128)(2,1)S(1)}, u32[]{:S(2)}, u32[]{:S(2)}) %collective-permute-start.11) | collective-permute-done | bytes 294944 | tf_op jit(solution)/shard_map/ppermute | solution.py:37
  174.2 1.7 collective-permute-start.29
  175.9 2.5 %shard_map.116 = bf16[128,3072]{1,0:T(8,128)(2,1)} custom-call(s32[2,128]{1,0:T(2,128)} %bitcast.49, f32[1,128]{1,0:T(1,128)} %bitcast.52, bf16[48,3072]{1,0:T(8,128)(2,1)} %get-tuple-element.37.own, bf16[48,3072]{1,0:T(8,128)(2,1)} %collective-permute-done.23.got), custom_call_target="tpu_custom_call" | custom-call | flops 37748736 | bytes 1400000 | tf_op jit(solution)/shard_map/pallas_call | solution.py:104
  178.4 2.5 %shard_map.113 = bf16[128,3072]{1,0:T(8,128)(2,1)} custom-call(s32[2,128]{1,0:T(2,128)} %bitcast.50, f32[1,128]{1,0:T(1,128)} %bitcast.53, bf16[48,3072]{1,0:T(8,128)(2,1)} %get-tuple-element.39.own, bf16[48,3072]{1,0:T(8,128)(2,1)} %copy-done.14), custom_call_target="tpu_custom_call" | custom-call | flops 37748736 | bytes 1400000 | tf_op jit(solution)/shard_map/pallas_call | solution.py:104
  180.9 1.9 add_convert_fusion.1
  182.9 1.0 collective-permute-start.36
  183.8 5.2 %collective-permute-done.27 = bf16[2,384,512]{2,1,0:T(8,128)(2,1)} collective-permute-done((bf16[2,384,512]{2,1,0:T(8,128)(2,1)}, bf16[2,384,512]{2,1,0:T(8,128)(2,1)}, u32[]{:S(2)}, u32[]{:S(2)}) %collective-permute-start.27) | collective-permute-done | bytes 786464 | tf_op jit(solution)/shard_map/ppermute | solution.py:37
  189.1 1.7 add_convert_fusion.2
  191.7 14.5 %collective-permute-done.40 = bf16[4,512,384]{2,1,0:T(8,128)(2,1)} collective-permute-done((bf16[4,512,384]{2,1,0:T(8,128)(2,1)}, bf16[4,512,384]{2,1,0:T(8,128)(2,1)}, u32[]{:S(2)}, u32[]{:S(2)}) %collective-permute-start.40) | collective-permute-done | bytes 1572896 | tf_op jit(solution)/shard_map/ppermute | solution.py:37
  206.2 1.8 add_convert_fusion
  208.2 2.7 %collective-permute-start.43 = (bf16[256,384]{1,0:T(8,128)(2,1)S(1)}, bf16[256,384]{1,0:T(8,128)(2,1)S(1)}, u32[]{:S(2)}, u32[]{:S(2)}) collective-permute-start(bf16[256,384]{1,0:T(8,128)(2,1)S(1)} %get-tuple-element.67), channel_id=1, source_target_pairs={{0,96},{1,97},{2,98},{3,99},{4,100},{5,101},{6,102},{7,103},{8,104... | collective-permute-start | bytes 589832 | tf_op jit(solution)/shard_map/ppermute | solution.py:37
  210.8 3.7 %collective-permute-done.36 = bf16[384,512]{1,0:T(8,128)(2,1)S(1)} collective-permute-done((bf16[384,512]{1,0:T(8,128)(2,1)S(1)}, bf16[384,512]{1,0:T(8,128)(2,1)S(1)}, u32[]{:S(2)}, u32[]{:S(2)}) %collective-permute-start.36) | collective-permute-done | bytes 393248 | tf_op jit(solution)/shard_map/ppermute | solution.py:37
  214.6 7.1 %collective-permute-start.37 = (bf16[192,512]{1,0:T(8,128)(2,1)S(1)}, bf16[192,512]{1,0:T(8,128)(2,1)S(1)}, u32[]{:S(2)}, u32[]{:S(2)}) collective-permute-start(bf16[192,512]{1,0:T(8,128)(2,1)S(1)} %broadcast_select_fusion.6), channel_id=1, source_target_pairs={{0,8},{1,9},{2,10},{3,11},{4,12},{5,13},{6,14},{7,15},{8,0},{9,1},... | collective-permute-start | bytes 589832 | tf_op jit(solution)/shard_map/ppermute | solution.py:37
  221.8 1.2 collective-permute-done.30
  223.1 3.8 %collective-permute-start.31 = (bf16[192,512]{1,0:T(8,128)(2,1)S(1)}, bf16[192,512]{1,0:T(8,128)(2,1)S(1)}, u32[]{:S(2)}, u32[]{:S(2)}) collective-permute-start(bf16[192,512]{1,0:T(8,128)(2,1)S(1)} %broadcast_select_fusion.10), channel_id=1, source_target_pairs={{0,8},{1,9},{2,10},{3,11},{4,12},{5,13},{6,14},{7,15},{8,0},{9,1},... | collective-permute-start | bytes 589832 | tf_op jit(solution)/shard_map/ppermute | solution.py:37
  227.2 2.7 %collective-permute-start.44 = (bf16[512,384]{1,0:T(8,128)(2,1)S(1)}, bf16[512,384]{1,0:T(8,128)(2,1)S(1)}, u32[]{:S(2)}, u32[]{:S(2)}) collective-permute-start(bf16[512,384]{1,0:T(8,128)(2,1)S(1)} %pad_maximum_fusion.12), channel_id=1, source_target_pairs={{0,96},{1,97},{2,98},{3,99},{4,100},{5,101},{6,102},{7,103},{8,104... | collective-permute-start | bytes 1179656 | tf_op jit(solution)/shard_map/ppermute | solution.py:37
  230.0 9.0 %collective-permute-done.42 = bf16[512,384]{1,0:T(8,128)(2,1)S(1)} collective-permute-done((bf16[512,384]{1,0:T(8,128)(2,1)S(1)}, bf16[512,384]{1,0:T(8,128)(2,1)S(1)}, u32[]{:S(2)}, u32[]{:S(2)}) %collective-permute-start.42) | collective-permute-done | bytes 393248 | tf_op jit(solution)/shard_map/ppermute | solution.py:37
  239.3 0.9 collective-permute-start.45
  242.1 0.9 copy.12
  (126 shorter events, 11.8 us)
Async XLA Ops:
  3.2 11.4 %collective-permute-start.2 = (bf16[48,3072]{1,0:T(8,128)(2,1)}, bf16[48,3072]{1,0:T(8,128)(2,1)S(1)}, u32[]{:S(2)}, u32[]{:S(2)}) collective-permute-start(bf16[48,3072]{1,0:T(8,128)(2,1)} %get-tuple-element.18.refs_6_), channel_id=1, source_target_pairs={{0,4},{1,5},{2,6},{3,7},{4,0},{5,1},{6,2},{7,3},{8,12},{9,13},{10,... | collective-permute-start | bytes 884744 | tf_op jit(solution)/shard_map/ppermute | solution.py:37
  7.7 9.7 %collective-permute-start = (bf16[48,3072]{1,0:T(8,128)(2,1)}, bf16[48,3072]{1,0:T(8,128)(2,1)S(1)}, u32[]{:S(2)}, u32[]{:S(2)}) collective-permute-start(bf16[48,3072]{1,0:T(8,128)(2,1)} %get-tuple-element.18.refs_6_), channel_id=1, source_target_pairs={{0,3},{1,0},{2,1},{3,2},{4,7},{5,4},{6,5},{7,6},{8,11},{9,8},{10,9... | collective-permute-start | bytes 884744 | tf_op jit(solution)/shard_map/ppermute | solution.py:37
  10.4 9.0 %collective-permute-start.6 = (bf16[48,3072]{1,0:T(8,128)(2,1)}, bf16[48,3072]{1,0:T(8,128)(2,1)S(1)}, u32[]{:S(2)}, u32[]{:S(2)}) collective-permute-start(bf16[48,3072]{1,0:T(8,128)(2,1)} %get-tuple-element.18.refs_6_), channel_id=1, source_target_pairs={{0,1},{1,2},{2,3},{3,0},{4,5},{5,6},{6,7},{7,4},{8,9},{9,10},{10,1... | collective-permute-start | bytes 884744 | tf_op jit(solution)/shard_map/ppermute | solution.py:37
  10.4 10.2 %collective-permute-start.14 = (bf16[48,3072]{1,0:T(8,128)(2,1)}, bf16[48,3072]{1,0:T(8,128)(2,1)S(1)}, u32[]{:S(2)}, u32[]{:S(2)}) collective-permute-start(bf16[48,3072]{1,0:T(8,128)(2,1)} %get-tuple-element.20.refs_6_), channel_id=1, source_target_pairs={{0,4},{1,5},{2,6},{3,7},{4,0},{5,1},{6,2},{7,3},{8,12},{9,13},{10,... | collective-permute-start | bytes 884744 | tf_op jit(solution)/shard_map/ppermute | solution.py:37
  14.6 23.4 %copy-start.16 = (bf16[48,3072]{1,0:T(8,128)(2,1)}, bf16[48,3072]{1,0:T(8,128)(2,1)S(1)}, u32[]{:S(2)}) copy-start(bf16[48,3072]{1,0:T(8,128)(2,1)S(1)} %collective-permute-done.2.refs_7_) | copy-start | bytes 884740
  14.6 10.8 %collective-permute-start.3 = (bf16[48,3072]{1,0:T(8,128)(2,1)S(1)}, bf16[48,3072]{1,0:T(8,128)(2,1)S(1)}, u32[]{:S(2)}, u32[]{:S(2)}) collective-permute-start(bf16[48,3072]{1,0:T(8,128)(2,1)S(1)} %collective-permute-done.2.refs_7_), channel_id=1, source_target_pairs={{0,1},{1,2},{2,3},{3,0},{4,5},{5,6},{6,7},{7,4},{8,9},{9,10},{10,1... | collective-permute-start | bytes 884744 | tf_op jit(solution)/shard_map/ppermute | solution.py:37
  15.9 10.7 %collective-permute-start.12 = (bf16[48,3072]{1,0:T(8,128)(2,1)}, bf16[48,3072]{1,0:T(8,128)(2,1)S(1)}, u32[]{:S(2)}, u32[]{:S(2)}) collective-permute-start(bf16[48,3072]{1,0:T(8,128)(2,1)} %get-tuple-element.20.refs_6_), channel_id=1, source_target_pairs={{0,3},{1,0},{2,1},{3,2},{4,7},{5,4},{6,5},{7,6},{8,11},{9,8},{10,9... | collective-permute-start | bytes 884744 | tf_op jit(solution)/shard_map/ppermute | solution.py:37
  17.3 20.7 %copy-start.17 = (bf16[48,3072]{1,0:T(8,128)(2,1)}, bf16[48,3072]{1,0:T(8,128)(2,1)S(1)}, u32[]{:S(2)}) copy-start(bf16[48,3072]{1,0:T(8,128)(2,1)S(1)} %collective-permute-done.refs_2_) | copy-start | bytes 884740
  17.4 11.2 %collective-permute-start.5 = (bf16[48,3072]{1,0:T(8,128)(2,1)S(1)}, bf16[48,3072]{1,0:T(8,128)(2,1)S(1)}, u32[]{:S(2)}, u32[]{:S(2)}) collective-permute-start(bf16[48,3072]{1,0:T(8,128)(2,1)S(1)} %collective-permute-done.2.refs_7_), channel_id=1, source_target_pairs={{0,3},{1,0},{2,1},{3,2},{4,7},{5,4},{6,5},{7,6},{8,11},{9,8},{10,9... | collective-permute-start | bytes 884744 | tf_op jit(solution)/shard_map/ppermute | solution.py:37
  19.4 18.7 %copy-start.18 = (bf16[48,3072]{1,0:T(8,128)(2,1)}, bf16[48,3072]{1,0:T(8,128)(2,1)S(1)}, u32[]{:S(2)}) copy-start(bf16[48,3072]{1,0:T(8,128)(2,1)S(1)} %collective-permute-done.6.refs_4_) | copy-start | bytes 884740
  19.4 15.5 %collective-permute-start.1 = (bf16[48,3072]{1,0:T(8,128)(2,1)S(1)}, bf16[48,3072]{1,0:T(8,128)(2,1)S(1)}, u32[]{:S(2)}, u32[]{:S(2)}) collective-permute-start(bf16[48,3072]{1,0:T(8,128)(2,1)S(1)} %collective-permute-done.refs_2_), channel_id=1, source_target_pairs={{0,3},{1,0},{2,1},{3,2},{4,7},{5,4},{6,5},{7,6},{8,11},{9,8},{10,9... | collective-permute-start | bytes 884744 | tf_op jit(solution)/shard_map/ppermute | solution.py:37
  20.6 29.6 %copy-start.6 = (bf16[48,3072]{1,0:T(8,128)(2,1)}, bf16[48,3072]{1,0:T(8,128)(2,1)S(1)}, u32[]{:S(2)}) copy-start(bf16[48,3072]{1,0:T(8,128)(2,1)S(1)} %collective-permute-done.14.refs_7_) | copy-start | bytes 884740
  20.6 17.3 %collective-permute-start.15 = (bf16[48,3072]{1,0:T(8,128)(2,1)S(1)}, bf16[48,3072]{1,0:T(8,128)(2,1)S(1)}, u32[]{:S(2)}, u32[]{:S(2)}) collective-permute-start(bf16[48,3072]{1,0:T(8,128)(2,1)S(1)} %collective-permute-done.14.refs_7_), channel_id=1, source_target_pairs={{0,1},{1,2},{2,3},{3,0},{4,5},{5,6},{6,7},{7,4},{8,9},{9,10},{10,1... | collective-permute-start | bytes 884744 | tf_op jit(solution)/shard_map/ppermute | solution.py:37
  25.4 12.7 %copy-start.19 = (bf16[48,3072]{1,0:T(8,128)(2,1)}, bf16[48,3072]{1,0:T(8,128)(2,1)S(1)}, u32[]{:S(2)}) copy-start(bf16[48,3072]{1,0:T(8,128)(2,1)S(1)} %collective-permute-done.3.refs_5_) | copy-start | bytes 884740
  25.4 12.6 %collective-permute-start.4 = (bf16[48,3072]{1,0:T(8,128)(2,1)S(1)}, bf16[48,3072]{1,0:T(8,128)(2,1)S(1)}, u32[]{:S(2)}, u32[]{:S(2)}) collective-permute-start(bf16[48,3072]{1,0:T(8,128)(2,1)S(1)} %collective-permute-done.3.refs_5_), channel_id=1, source_target_pairs={{0,1},{1,2},{2,3},{3,0},{4,5},{5,6},{6,7},{7,4},{8,9},{9,10},{10,1... | collective-permute-start | bytes 884744 | tf_op jit(solution)/shard_map/ppermute | solution.py:37
  26.6 23.6 %copy-start.7 = (bf16[48,3072]{1,0:T(8,128)(2,1)}, bf16[48,3072]{1,0:T(8,128)(2,1)S(1)}, u32[]{:S(2)}) copy-start(bf16[48,3072]{1,0:T(8,128)(2,1)S(1)} %collective-permute-done.12.refs_2_) | copy-start | bytes 884740
  26.6 23.7 %collective-permute-start.18 = (bf16[48,3072]{1,0:T(8,128)(2,1)}, bf16[48,3072]{1,0:T(8,128)(2,1)S(1)}, u32[]{:S(2)}, u32[]{:S(2)}) collective-permute-start(bf16[48,3072]{1,0:T(8,128)(2,1)} %get-tuple-element.20.refs_6_), channel_id=1, source_target_pairs={{0,1},{1,2},{2,3},{3,0},{4,5},{5,6},{6,7},{7,4},{8,9},{9,10},{10,1... | collective-permute-start | bytes 884744 | tf_op jit(solution)/shard_map/ppermute | solution.py:37
  28.6 9.5 %copy-start.20 = (bf16[48,3072]{1,0:T(8,128)(2,1)}, bf16[48,3072]{1,0:T(8,128)(2,1)S(1)}, u32[]{:S(2)}) copy-start(bf16[48,3072]{1,0:T(8,128)(2,1)S(1)} %collective-permute-done.5.refs_3_) | copy-start | bytes 884740
  28.6 21.7 %collective-permute-start.17 = (bf16[48,3072]{1,0:T(8,128)(2,1)S(1)}, bf16[48,3072]{1,0:T(8,128)(2,1)S(1)}, u32[]{:S(2)}, u32[]{:S(2)}) collective-permute-start(bf16[48,3072]{1,0:T(8,128)(2,1)S(1)} %collective-permute-done.14.refs_7_), channel_id=1, source_target_pairs={{0,3},{1,0},{2,1},{3,2},{4,7},{5,4},{6,5},{7,6},{8,11},{9,8},{10,9... | collective-permute-start | bytes 884744 | tf_op jit(solution)/shard_map/ppermute | solution.py:37
  34.9 3.2 %copy-start.21 = (bf16[48,3072]{1,0:T(8,128)(2,1)}, bf16[48,3072]{1,0:T(8,128)(2,1)S(1)}, u32[]{:S(2)}) copy-start(bf16[48,3072]{1,0:T(8,128)(2,1)S(1)} %collective-permute-done.1.refs_0_) | copy-start | bytes 884740
  34.9 15.4 %collective-permute-start.13 = (bf16[48,3072]{1,0:T(8,128)(2,1)S(1)}, bf16[48,3072]{1,0:T(8,128)(2,1)S(1)}, u32[]{:S(2)}, u32[]{:S(2)}) collective-permute-start(bf16[48,3072]{1,0:T(8,128)(2,1)S(1)} %collective-permute-done.12.refs_2_), channel_id=1, source_target_pairs={{0,3},{1,0},{2,1},{3,2},{4,7},{5,4},{6,5},{7,6},{8,11},{9,8},{10,9... | collective-permute-start | bytes 884744 | tf_op jit(solution)/shard_map/ppermute | solution.py:37
  37.9 12.3 %copy-start.8 = (bf16[48,3072]{1,0:T(8,128)(2,1)}, bf16[48,3072]{1,0:T(8,128)(2,1)S(1)}, u32[]{:S(2)}) copy-start(bf16[48,3072]{1,0:T(8,128)(2,1)S(1)} %collective-permute-done.15.refs_5_) | copy-start | bytes 884740
  37.9 12.6 %collective-permute-start.16 = (bf16[48,3072]{1,0:T(8,128)(2,1)S(1)}, bf16[48,3072]{1,0:T(8,128)(2,1)S(1)}, u32[]{:S(2)}, u32[]{:S(2)}) collective-permute-start(bf16[48,3072]{1,0:T(8,128)(2,1)S(1)} %collective-permute-done.15.refs_5_), channel_id=1, source_target_pairs={{0,1},{1,2},{2,3},{3,0},{4,5},{5,6},{6,7},{7,4},{8,9},{9,10},{10,1... | collective-permute-start | bytes 884744 | tf_op jit(solution)/shard_map/ppermute | solution.py:37
  51.3 14.8 %copy-start.15 = (bf16[384,3072]{1,0:T(8,128)(2,1)S(1)}, bf16[384,3072]{1,0:T(8,128)(2,1)}, u32[]{:S(2)}) copy-start(bf16[384,3072]{1,0:T(8,128)(2,1)} %get-tuple-element.25.x_own) | copy-start | bytes 7077892
  60.3 91.6 %collective-permute-start.38 = (bf16[384,3072]{1,0:T(8,128)(2,1)}, bf16[384,3072]{1,0:T(8,128)(2,1)S(1)}, u32[]{:S(2)}, u32[]{:S(2)}) collective-permute-start(bf16[384,3072]{1,0:T(8,128)(2,1)} %get-tuple-element.29.d_own), channel_id=1, source_target_pairs={{0,8},{1,9},{2,10},{3,11},{4,12},{5,13},{6,14},{7,15},{8,0},{9,1},... | collective-permute-start | bytes 7077896 | tf_op jit(solution)/shard_map/ppermute | solution.py:37
  66.0 50.3 %collective-permute-start.25 = (bf16[2,384,512]{2,1,0:T(8,128)(2,1)}, bf16[2,384,512]{2,1,0:T(8,128)(2,1)}, u32[]{:S(2)}, u32[]{:S(2)}) collective-permute-start(bf16[2,384,512]{2,1,0:T(8,128)(2,1)} %get-tuple-element.26), channel_id=1, source_target_pairs={{0,8},{1,9},{2,10},{3,11},{4,12},{5,13},{6,14},{7,15},{8,0},{9,1},... | collective-permute-start | bytes 2359304 | tf_op jit(solution)/shard_map/ppermute | solution.py:37
  66.1 52.9 %collective-permute-start.24 = (bf16[384,3072]{1,0:T(8,128)(2,1)S(1)}, bf16[384,3072]{1,0:T(8,128)(2,1)}, u32[]{:S(2)}, u32[]{:S(2)}) collective-permute-start(bf16[384,3072]{1,0:T(8,128)(2,1)S(1)} %copy-done.15), channel_id=1, source_target_pairs={{0,8},{1,9},{2,10},{3,11},{4,12},{5,13},{6,14},{7,15},{8,0},{9,1},... | collective-permute-start | bytes 7077896 | tf_op jit(solution)/shard_map/ppermute | solution.py:37
  77.5 11.2 %collective-permute-start.19 = (bf16[48,3072]{1,0:T(8,128)(2,1)S(1)}, bf16[48,3072]{1,0:T(8,128)(2,1)S(1)}, u32[]{:S(2)}, u32[]{:S(2)}) collective-permute-start(bf16[48,3072]{1,0:T(8,128)(2,1)S(1)} %get-tuple-element.54), channel_id=1, source_target_pairs={{0,1},{1,2},{2,3},{3,0},{4,5},{5,6},{6,7},{7,4},{8,9},{9,10},{10,1... | collective-permute-start | bytes 884744 | tf_op jit(solution)/shard_map/ppermute | solution.py:37
  78.3 10.5 %collective-permute-start.21 = (bf16[48,3072]{1,0:T(8,128)(2,1)S(1)}, bf16[48,3072]{1,0:T(8,128)(2,1)S(1)}, u32[]{:S(2)}, u32[]{:S(2)}) collective-permute-start(bf16[48,3072]{1,0:T(8,128)(2,1)S(1)} %get-tuple-element.55), channel_id=1, source_target_pairs={{0,3},{1,0},{2,1},{3,2},{4,7},{5,4},{6,5},{7,6},{8,11},{9,8},{10,9... | collective-permute-start | bytes 884744 | tf_op jit(solution)/shard_map/ppermute | solution.py:37
  87.3 4.2 %copy-start.4 = (bf16[384,3072]{1,0:T(8,128)(2,1)S(1)}, bf16[384,3072]{1,0:T(8,128)(2,1)}, u32[]{:S(2)}) copy-start(bf16[384,3072]{1,0:T(8,128)(2,1)} %shard_map.115) | copy-start | bytes 7077892
  88.7 9.5 %collective-permute-start.7 = (bf16[48,3072]{1,0:T(8,128)(2,1)S(1)}, bf16[48,3072]{1,0:T(8,128)(2,1)S(1)}, u32[]{:S(2)}, u32[]{:S(2)}) collective-permute-start(bf16[48,3072]{1,0:T(8,128)(2,1)S(1)} %get-tuple-element.60), channel_id=1, source_target_pairs={{0,1},{1,2},{2,3},{3,0},{4,5},{5,6},{6,7},{7,4},{8,9},{9,10},{10,1... | collective-permute-start | bytes 884744 | tf_op jit(solution)/shard_map/ppermute | solution.py:37
  88.8 9.4 %collective-permute-start.9 = (bf16[48,3072]{1,0:T(8,128)(2,1)S(1)}, bf16[48,3072]{1,0:T(8,128)(2,1)S(1)}, u32[]{:S(2)}, u32[]{:S(2)}) collective-permute-start(bf16[48,3072]{1,0:T(8,128)(2,1)S(1)} %get-tuple-element.61), channel_id=1, source_target_pairs={{0,3},{1,0},{2,1},{3,2},{4,7},{5,4},{6,5},{7,6},{8,11},{9,8},{10,9... | collective-permute-start | bytes 884744 | tf_op jit(solution)/shard_map/ppermute | solution.py:37
  91.6 9.3 %copy-start.1 = (bf16[384,3072]{1,0:T(8,128)(2,1)S(1)}, bf16[384,3072]{1,0:T(8,128)(2,1)}, u32[]{:S(2)}) copy-start(bf16[384,3072]{1,0:T(8,128)(2,1)} %shard_map.112) | copy-start | bytes 7077892
  98.3 14.8 %collective-permute-start.20 = (bf16[96,3072]{1,0:T(8,128)(2,1)S(1)}, bf16[96,3072]{1,0:T(8,128)(2,1)S(1)}, u32[]{:S(2)}, u32[]{:S(2)}) collective-permute-start(bf16[96,3072]{1,0:T(8,128)(2,1)S(1)} %pad_maximum_fusion.6), channel_id=1, source_target_pairs={{0,1},{1,2},{2,3},{3,0},{4,5},{5,6},{6,7},{7,4},{8,9},{9,10},{10,1... | collective-permute-start | bytes 1769480 | tf_op jit(solution)/shard_map/ppermute | solution.py:37
  98.3 17.0 %collective-permute-start.22 = (bf16[96,3072]{1,0:T(8,128)(2,1)S(1)}, bf16[96,3072]{1,0:T(8,128)(2,1)S(1)}, u32[]{:S(2)}, u32[]{:S(2)}) collective-permute-start(bf16[96,3072]{1,0:T(8,128)(2,1)S(1)} %pad_maximum_fusion.7), channel_id=1, source_target_pairs={{0,3},{1,0},{2,1},{3,2},{4,7},{5,4},{6,5},{7,6},{8,11},{9,8},{10,9... | collective-permute-start | bytes 1769480 | tf_op jit(solution)/shard_map/ppermute | solution.py:37
  113.1 38.8 %collective-permute-start.39 = (bf16[384,512]{1,0:T(8,128)(2,1)}, bf16[384,512]{1,0:T(8,128)(2,1)S(1)}, u32[]{:S(2)}, u32[]{:S(2)}) collective-permute-start(bf16[384,512]{1,0:T(8,128)(2,1)} %get-tuple-element.30), channel_id=1, source_target_pairs={{0,8},{1,9},{2,10},{3,11},{4,12},{5,13},{6,14},{7,15},{8,0},{9,1},... | collective-permute-start | bytes 1179656 | tf_op jit(solution)/shard_map/ppermute | solution.py:37
  115.2 19.7 %collective-permute-start.8 = (bf16[96,3072]{1,0:T(8,128)(2,1)}, bf16[96,3072]{1,0:T(8,128)(2,1)}, u32[]{:S(2)}, u32[]{:S(2)}) collective-permute-start(bf16[96,3072]{1,0:T(8,128)(2,1)} %pad_maximum_fusion.4), channel_id=1, source_target_pairs={{0,1},{1,2},{2,3},{3,0},{4,5},{5,6},{6,7},{7,4},{8,9},{9,10},{10,1... | collective-permute-start | bytes 1769480 | tf_op jit(solution)/shard_map/ppermute | solution.py:37
  116.2 20.0 %collective-permute-start.10 = (bf16[96,3072]{1,0:T(8,128)(2,1)}, bf16[96,3072]{1,0:T(8,128)(2,1)}, u32[]{:S(2)}, u32[]{:S(2)}) collective-permute-start(bf16[96,3072]{1,0:T(8,128)(2,1)} %pad_maximum_fusion.5), channel_id=1, source_target_pairs={{0,3},{1,0},{2,1},{3,2},{4,7},{5,4},{6,5},{7,6},{8,11},{9,8},{10,9... | collective-permute-start | bytes 1769480 | tf_op jit(solution)/shard_map/ppermute | solution.py:37
  118.9 51.3 %collective-permute-start.23 = (bf16[48,3072]{1,0:T(8,128)(2,1)}, bf16[48,3072]{1,0:T(8,128)(2,1)}, u32[]{:S(2)}, u32[]{:S(2)}) collective-permute-start(bf16[48,3072]{1,0:T(8,128)(2,1)} %get-tuple-element.36), channel_id=1, source_target_pairs={{0,4},{1,5},{2,6},{3,7},{4,0},{5,1},{6,2},{7,3},{8,12},{9,13},{10,... | collective-permute-start | bytes 884744 | tf_op jit(solution)/shard_map/ppermute | solution.py:37
  133.3 6.6 %copy-start.2 = (bf16[8,384,512]{2,1,0:T(8,128)(2,1)S(1)}, bf16[8,384,512]{2,1,0:T(8,128)(2,1)}, u32[]{:S(2)}) copy-start(bf16[8,384,512]{2,1,0:T(8,128)(2,1)} %get-tuple-element.27) | copy-start | bytes 9437188
  134.9 11.1 %collective-permute-start.32 = (bf16[1,384,512]{2,1,0:T(8,128)(2,1)S(1)}, bf16[1,384,512]{2,1,0:T(8,128)(2,1)S(1)}, u32[]{:S(2)}, u32[]{:S(2)}) collective-permute-start(bf16[1,384,512]{2,1,0:T(8,128)(2,1)S(1)} %get-tuple-element.42), channel_id=1, source_target_pairs={{0,32},{1,33},{2,34},{3,35},{4,36},{5,37},{6,38},{7,39},{8,40},{9,... | collective-permute-start | bytes 1179656 | tf_op jit(solution)/shard_map/ppermute | solution.py:37
  136.2 9.8 %collective-permute-start.34 = (bf16[1,384,512]{2,1,0:T(8,128)(2,1)S(1)}, bf16[1,384,512]{2,1,0:T(8,128)(2,1)S(1)}, u32[]{:S(2)}, u32[]{:S(2)}) collective-permute-start(bf16[1,384,512]{2,1,0:T(8,128)(2,1)S(1)} %get-tuple-element.43), channel_id=1, source_target_pairs={{0,96},{1,97},{2,98},{3,99},{4,100},{5,101},{6,102},{7,103},{8,104... | collective-permute-start | bytes 1179656 | tf_op jit(solution)/shard_map/ppermute | solution.py:37
  146.0 21.1 %collective-permute-start.26 = (bf16[1,384,512]{2,1,0:T(8,128)(2,1)S(1)}, bf16[1,384,512]{2,1,0:T(8,128)(2,1)S(1)}, u32[]{:S(2)}, u32[]{:S(2)}) collective-permute-start(bf16[1,384,512]{2,1,0:T(8,128)(2,1)S(1)} %get-tuple-element.48), channel_id=1, source_target_pairs={{0,32},{1,33},{2,34},{3,35},{4,36},{5,37},{6,38},{7,39},{8,40},{9,... | collective-permute-start | bytes 1179656 | tf_op jit(solution)/shard_map/ppermute | solution.py:37
  146.0 21.4 %collective-permute-start.28 = (bf16[1,384,512]{2,1,0:T(8,128)(2,1)S(1)}, bf16[1,384,512]{2,1,0:T(8,128)(2,1)S(1)}, u32[]{:S(2)}, u32[]{:S(2)}) collective-permute-start(bf16[1,384,512]{2,1,0:T(8,128)(2,1)S(1)} %get-tuple-element.49), channel_id=1, source_target_pairs={{0,96},{1,97},{2,98},{3,99},{4,100},{5,101},{6,102},{7,103},{8,104... | collective-permute-start | bytes 1179656 | tf_op jit(solution)/shard_map/ppermute | solution.py:37
  151.9 2.7 %copy-start.5 = (bf16[384,512]{1,0:T(8,128)(2,1)}, bf16[384,512]{1,0:T(8,128)(2,1)S(1)}, u32[]{:S(2)}) copy-start(bf16[384,512]{1,0:T(8,128)(2,1)S(1)} %collective-permute-done.39.h_other) | copy-start | bytes 1179652
  151.9 29.0 %collective-permute-start.33 = (bf16[2,384,512]{2,1,0:T(8,128)(2,1)}, bf16[2,384,512]{2,1,0:T(8,128)(2,1)}, u32[]{:S(2)}, u32[]{:S(2)}) collective-permute-start(bf16[2,384,512]{2,1,0:T(8,128)(2,1)} %pad_maximum_fusion.2), channel_id=1, source_target_pairs={{0,32},{1,33},{2,34},{3,35},{4,36},{5,37},{6,38},{7,39},{8,40},{9,... | collective-permute-start | bytes 2359304 | tf_op jit(solution)/shard_map/ppermute | solution.py:37
  152.0 2.7 %copy-start.3 = (bf16[384,3072]{1,0:T(8,128)(2,1)}, bf16[384,3072]{1,0:T(8,128)(2,1)S(1)}, u32[]{:S(2)}) copy-start(bf16[384,3072]{1,0:T(8,128)(2,1)S(1)} %collective-permute-done.38.d_other) | copy-start | bytes 7077892
  152.0 29.0 %collective-permute-start.35 = (bf16[2,384,512]{2,1,0:T(8,128)(2,1)}, bf16[2,384,512]{2,1,0:T(8,128)(2,1)}, u32[]{:S(2)}, u32[]{:S(2)}) collective-permute-start(bf16[2,384,512]{2,1,0:T(8,128)(2,1)} %pad_maximum_fusion.3), channel_id=1, source_target_pairs={{0,96},{1,97},{2,98},{3,99},{4,100},{5,101},{6,102},{7,103},{8,104... | collective-permute-start | bytes 2359304 | tf_op jit(solution)/shard_map/ppermute | solution.py:37
  164.3 2.8 %copy-start.9 = (bf16[48,3072]{1,0:T(8,128)(2,1)S(1)}, bf16[48,3072]{1,0:T(8,128)(2,1)}, u32[]{:S(2)}) copy-start(bf16[48,3072]{1,0:T(8,128)(2,1)} %get-tuple-element.38) | copy-start | bytes 884740
  167.1 7.1 %collective-permute-start.11 = (bf16[48,3072]{1,0:T(8,128)(2,1)S(1)}, bf16[48,3072]{1,0:T(8,128)(2,1)S(1)}, u32[]{:S(2)}, u32[]{:S(2)}) collective-permute-start(bf16[48,3072]{1,0:T(8,128)(2,1)S(1)} %copy-done.9), channel_id=1, source_target_pairs={{0,4},{1,5},{2,6},{3,7},{4,0},{5,1},{6,2},{7,3},{8,12},{9,13},{10,... | collective-permute-start | bytes 884744 | tf_op jit(solution)/shard_map/ppermute | solution.py:37
  167.4 38.8 %collective-permute-start.40 = (bf16[4,512,384]{2,1,0:T(8,128)(2,1)}, bf16[4,512,384]{2,1,0:T(8,128)(2,1)}, u32[]{:S(2)}, u32[]{:S(2)}) collective-permute-start(bf16[4,512,384]{2,1,0:T(8,128)(2,1)} %slice.233), channel_id=1, source_target_pairs={{0,16},{1,17},{2,18},{3,19},{4,20},{5,21},{6,22},{7,23},{8,24},{9,... | collective-permute-start | bytes 4718600 | tf_op jit(solution)/shard_map/ppermute | solution.py:37
  170.3 18.8 %collective-permute-start.27 = (bf16[2,384,512]{2,1,0:T(8,128)(2,1)}, bf16[2,384,512]{2,1,0:T(8,128)(2,1)}, u32[]{:S(2)}, u32[]{:S(2)}) collective-permute-start(bf16[2,384,512]{2,1,0:T(8,128)(2,1)} %pad_maximum_fusion), channel_id=1, source_target_pairs={{0,32},{1,33},{2,34},{3,35},{4,36},{5,37},{6,38},{7,39},{8,40},{9,... | collective-permute-start | bytes 2359304 | tf_op jit(solution)/shard_map/ppermute | solution.py:37
  174.2 4.2 %copy-start.14 = (bf16[48,3072]{1,0:T(8,128)(2,1)}, bf16[48,3072]{1,0:T(8,128)(2,1)S(1)}, u32[]{:S(2)}) copy-start(bf16[48,3072]{1,0:T(8,128)(2,1)S(1)} %collective-permute-done.11.got) | copy-start | bytes 884740
  174.2 14.9 %collective-permute-start.29 = (bf16[2,384,512]{2,1,0:T(8,128)(2,1)}, bf16[2,384,512]{2,1,0:T(8,128)(2,1)}, u32[]{:S(2)}, u32[]{:S(2)}) collective-permute-start(bf16[2,384,512]{2,1,0:T(8,128)(2,1)} %pad_maximum_fusion.1), channel_id=1, source_target_pairs={{0,96},{1,97},{2,98},{3,99},{4,100},{5,101},{6,102},{7,103},{8,104... | collective-permute-start | bytes 2359304 | tf_op jit(solution)/shard_map/ppermute | solution.py:37
  182.9 23.3 %copy-start = (bf16[8,512,384]{2,1,0:T(8,128)(2,1)S(1)}, bf16[8,512,384]{2,1,0:T(8,128)(2,1)}, u32[]{:S(2)}) copy-start(bf16[8,512,384]{2,1,0:T(8,128)(2,1)} %shard_map.118) | copy-start | bytes 9437188
  182.9 31.6 %collective-permute-start.36 = (bf16[384,512]{1,0:T(8,128)(2,1)S(1)}, bf16[384,512]{1,0:T(8,128)(2,1)S(1)}, u32[]{:S(2)}, u32[]{:S(2)}) collective-permute-start(bf16[384,512]{1,0:T(8,128)(2,1)S(1)} %slice_bitcast_fusion.1), channel_id=1, source_target_pairs={{0,16},{1,17},{2,18},{3,19},{4,20},{5,21},{6,22},{7,23},{8,24},{9,... | collective-permute-start | bytes 1179656 | tf_op jit(solution)/shard_map/ppermute | solution.py:37
  190.8 32.1 %collective-permute-start.30 = (bf16[384,512]{1,0:T(8,128)(2,1)S(1)}, bf16[384,512]{1,0:T(8,128)(2,1)S(1)}, u32[]{:S(2)}, u32[]{:S(2)}) collective-permute-start(bf16[384,512]{1,0:T(8,128)(2,1)S(1)} %slice_bitcast_fusion.3), channel_id=1, source_target_pairs={{0,16},{1,17},{2,18},{3,19},{4,20},{5,21},{6,22},{7,23},{8,24},{9,... | collective-permute-start | bytes 1179656 | tf_op jit(solution)/shard_map/ppermute | solution.py:37
  208.1 18.8 %collective-permute-start.41 = (bf16[256,384]{1,0:T(8,128)(2,1)S(1)}, bf16[256,384]{1,0:T(8,128)(2,1)S(1)}, u32[]{:S(2)}, u32[]{:S(2)}) collective-permute-start(bf16[256,384]{1,0:T(8,128)(2,1)S(1)} %get-tuple-element.66), channel_id=1, source_target_pairs={{0,32},{1,33},{2,34},{3,35},{4,36},{5,37},{6,38},{7,39},{8,40},{9,... | collective-permute-start | bytes 589832 | tf_op jit(solution)/shard_map/ppermute | solution.py:37
  208.2 18.7 %collective-permute-start.43 = (bf16[256,384]{1,0:T(8,128)(2,1)S(1)}, bf16[256,384]{1,0:T(8,128)(2,1)S(1)}, u32[]{:S(2)}, u32[]{:S(2)}) collective-permute-start(bf16[256,384]{1,0:T(8,128)(2,1)S(1)} %get-tuple-element.67), channel_id=1, source_target_pairs={{0,96},{1,97},{2,98},{3,99},{4,100},{5,101},{6,102},{7,103},{8,104... | collective-permute-start | bytes 589832 | tf_op jit(solution)/shard_map/ppermute | solution.py:37
  214.6 15.3 %collective-permute-start.37 = (bf16[192,512]{1,0:T(8,128)(2,1)S(1)}, bf16[192,512]{1,0:T(8,128)(2,1)S(1)}, u32[]{:S(2)}, u32[]{:S(2)}) collective-permute-start(bf16[192,512]{1,0:T(8,128)(2,1)S(1)} %broadcast_select_fusion.6), channel_id=1, source_target_pairs={{0,8},{1,9},{2,10},{3,11},{4,12},{5,13},{6,14},{7,15},{8,0},{9,1},... | collective-permute-start | bytes 589832 | tf_op jit(solution)/shard_map/ppermute | solution.py:37
  223.1 6.9 %collective-permute-start.31 = (bf16[192,512]{1,0:T(8,128)(2,1)S(1)}, bf16[192,512]{1,0:T(8,128)(2,1)S(1)}, u32[]{:S(2)}, u32[]{:S(2)}) collective-permute-start(bf16[192,512]{1,0:T(8,128)(2,1)S(1)} %broadcast_select_fusion.10), channel_id=1, source_target_pairs={{0,8},{1,9},{2,10},{3,11},{4,12},{5,13},{6,14},{7,15},{8,0},{9,1},... | collective-permute-start | bytes 589832 | tf_op jit(solution)/shard_map/ppermute | solution.py:37
  227.0 12.0 %collective-permute-start.42 = (bf16[512,384]{1,0:T(8,128)(2,1)S(1)}, bf16[512,384]{1,0:T(8,128)(2,1)S(1)}, u32[]{:S(2)}, u32[]{:S(2)}) collective-permute-start(bf16[512,384]{1,0:T(8,128)(2,1)S(1)} %pad_maximum_fusion.11), channel_id=1, source_target_pairs={{0,32},{1,33},{2,34},{3,35},{4,36},{5,37},{6,38},{7,39},{8,40},{9,... | collective-permute-start | bytes 1179656 | tf_op jit(solution)/shard_map/ppermute | solution.py:37
  227.2 11.9 %collective-permute-start.44 = (bf16[512,384]{1,0:T(8,128)(2,1)S(1)}, bf16[512,384]{1,0:T(8,128)(2,1)S(1)}, u32[]{:S(2)}, u32[]{:S(2)}) collective-permute-start(bf16[512,384]{1,0:T(8,128)(2,1)S(1)} %pad_maximum_fusion.12), channel_id=1, source_target_pairs={{0,96},{1,97},{2,98},{3,99},{4,100},{5,101},{6,102},{7,103},{8,104... | collective-permute-start | bytes 1179656 | tf_op jit(solution)/shard_map/ppermute | solution.py:37
  239.3 2.5 %collective-permute-start.45 = (bf16[512,192]{1,0:T(8,128)(2,1)S(1)}, bf16[512,192]{1,0:T(8,128)(2,1)S(1)}, u32[]{:S(2)}, u32[]{:S(2)}) collective-permute-start(bf16[512,192]{1,0:T(8,128)(2,1)S(1)} %broadcast_select_fusion.2), channel_id=1, source_target_pairs={{0,8},{1,9},{2,10},{3,11},{4,12},{5,13},{6,14},{7,15},{8,0},{9,1},... | collective-permute-start | bytes 589832 | tf_op jit(solution)/shard_map/ppermute | solution.py:37
  (5 other events, 3.9 us)
